TPU v7x, 256 devices: a whole 4x4x8 slice. The times are simulated.
256 devices in a mesh: seq: 64 (over z_hi, y, x), red: 4 (over z_lo, core).
Axes of the slice: x: 4, y: 4, z: 8 (z_hi: 4, z_lo: 2; z = z_hi * 2 + z_lo), core: 2. Of those that a mesh axis runs over, the one named last changes fastest.
Arguments:
- token_ids: int32 [8192], P('seq'), may hold values from 0 to 511
- embedding: bfloat16 [512, 4096], P(None, 'red'), may hold values from -6 to 6
- proj_weight: bfloat16 [4096, 3, 4, 256], P('red', None, None, 'seq'), may hold values from -0.09375 to 0.09375
- filters: float32 [8192, 1024], P('seq', 'red'), may hold values from -1 to 1
- cotangent: float32 [8192, 1024], P('seq', 'red'), may hold values from -6 to 6
Outputs:
- output: float32 [8192, 1024], P('seq', 'red')
- filter_grad: float32 [8192, 1024], P('seq', 'red')
- branch_grads: bfloat16 [8192, 3, 1024], P('seq', None, 'red')
- weight_grad: float32 [4096, 3, 4, 256], P('red', None, None, 'seq')
All inputs are finite; a program needn't handle non-finite values.
Results may differ from a plain program's by a relative error of at most 0.0029.
Values sent between devices are 32-bit elements; how exact they have to be, the bound alone decides.
No kernel may reach another device: no remote copies, remote signals or barrier semaphores. Data moves between devices by JAX's collectives and lax.ppermute only.
A program may use at most 64 MiB of HBM per device.

v0:
```python
import math
import jax
import jax.numpy as jnp
from jax import lax
from jax.sharding import PartitionSpec as P

precise_mode = lax.Precision.HIGHEST


def in_blocks(value, dim, length):
    before, after = (value.shape[:dim], value.shape[dim + 1 :])
    return jnp.moveaxis(value.reshape(*before, length, -1, *after), dim, 0)


def summed_on_arrival(value, axis, dim):
    tiles = in_blocks(value, dim, lax.axis_size(axis))
    arrived = lax.all_to_all(tiles, axis, split_axis=0, concat_axis=0, tiled=True)
    return arrived.sum(axis=0)


def copy_for_each(value, axis):
    length = lax.axis_size(axis)
    return lax.all_to_all(
        jnp.broadcast_to(value[None], (length, *value.shape)), axis, 0, 0, tiled=True
    )


def in_order(tiles, dim):
    tiles = jnp.moveaxis(tiles, 0, dim)
    shape = tiles.shape
    return tiles.reshape(*shape[:dim], shape[dim] * shape[dim + 1], *shape[dim + 2 :])


def gather_directly(value, axis, dim):
    tiles = copy_for_each(value, axis)
    return in_order(tiles, dim)


def angles(numbers, modulus, direction):
    phase = (numbers % modulus).astype(jnp.float32) * (direction * 2.0 * math.pi / modulus)
    return (jnp.cos(phase), jnp.sin(phase))


def rotate(real_part, imag_part, cosine, sine_part):
    return (real_part * cosine - imag_part * sine_part, real_part * sine_part + imag_part * cosine)


def complex_einsum(formula, matrix, values):
    mat_real, mat_imag = matrix
    val_real, val_imag = values
    real_out = jnp.einsum(formula, mat_real, val_real, precision=precise_mode) - jnp.einsum(
        formula, mat_imag, val_imag, precision=precise_mode
    )
    imag_out = jnp.einsum(formula, mat_real, val_imag, precision=precise_mode) + jnp.einsum(
        formula, mat_imag, val_real, precision=precise_mode
    )
    return (real_out, imag_out)


def factors(length_total):
    first_factor = 1
    for candidate in range(1, math.isqrt(length_total) + 1):
        if length_total % candidate == 0:
            first_factor = candidate
    return (first_factor, length_total // first_factor)


def combine_spectra(spec_real, spec_imag, width):
    filt_re = spec_real[..., :width]
    inner_re = spec_real[..., width : 2 * width]
    up_re = spec_real[..., 2 * width :]
    filt_im = spec_imag[..., :width]
    inner_im = spec_imag[..., width : 2 * width]
    up_im = spec_imag[..., 2 * width :]
    joined_real = jnp.concatenate(
        [
            filt_re * inner_re - filt_im * inner_im,
            filt_re * up_re + filt_im * up_im,
            up_re * inner_re + up_im * inner_im,
        ],
        axis=-1,
    )
    joined_imag = jnp.concatenate(
        [
            filt_re * inner_im + filt_im * inner_re,
            filt_re * up_im - filt_im * up_re,
            up_im * inner_re - up_re * inner_im,
        ],
        axis=-1,
    )
    return (joined_real, joined_imag)


def local_convolve(signals):
    length, branch_count, narrow = signals.shape
    total = 2 * length
    first_factor, second_factor = factors(total)
    flat = signals.reshape(length, branch_count * narrow)
    padded = jnp.concatenate([flat, jnp.zeros_like(flat)], axis=0).reshape(
        first_factor, second_factor, branch_count * narrow
    )
    first_index = jnp.arange(first_factor, dtype=jnp.int32)
    second_index = jnp.arange(second_factor, dtype=jnp.int32)
    cosine, sine_part = angles(first_index[:, None] * first_index[None, :], first_factor, -1.0)
    real_part = jnp.einsum("kn,nbm->kbm", cosine, padded, precision=precise_mode)
    imag_part = jnp.einsum("kn,nbm->kbm", sine_part, padded, precision=precise_mode)
    cosine, sine_part = angles(first_index[:, None] * second_index[None, :], total, -1.0)
    real_part, imag_part = rotate(real_part, imag_part, cosine[:, :, None], sine_part[:, :, None])
    real_part, imag_part = complex_einsum(
        "lb,kbm->klm",
        angles(second_index[:, None] * second_index[None, :], second_factor, -1.0),
        (real_part, imag_part),
    )
    real_part, imag_part = combine_spectra(real_part, imag_part, narrow)
    real_part, imag_part = complex_einsum(
        "bl,klm->kbm",
        angles(second_index[:, None] * second_index[None, :], second_factor, 1.0),
        (real_part, imag_part),
    )
    cosine, sine_part = angles(first_index[:, None] * second_index[None, :], total, 1.0)
    real_part, imag_part = rotate(real_part, imag_part, cosine[:, :, None], sine_part[:, :, None])
    cosine, sine_part = angles(first_index[:, None] * first_index[None, :], first_factor, 1.0)
    result = jnp.einsum("nk,kbm->nbm", cosine, real_part, precision=precise_mode) - jnp.einsum(
        "nk,kbm->nbm", sine_part, imag_part, precision=precise_mode
    )
    result = result.reshape(total, branch_count * narrow)[:length] / total
    return result.reshape(length, branch_count, narrow)


def shards(token_ids, embedding, proj_weight, filters, cotangent):
    tok_count = token_ids.shape[0]
    devices = lax.axis_size("seq")
    width = filters.shape[1]
    vocabulary = embedding.shape[0]
    width_rows, branches, red_count, piece = proj_weight.shape
    scale_factor = float(tok_count * devices) ** (-0.5)
    table = jnp.dot(
        embedding,
        proj_weight.reshape(width_rows, branches * red_count * piece),
        preferred_element_type=jnp.float32,
    )
    table = table.reshape(vocabulary, branches, red_count, piece)
    own_table = summed_on_arrival(table, "red", 2)
    full_table = gather_directly(own_table, "seq", 3)
    projected = jnp.take(full_table, token_ids, axis=0)
    projected = projected.reshape(tok_count, branches, width)
    queries = projected[:, 0]
    key_rows = projected[:, 1]
    value_rows = projected[:, 2]
    inner = key_rows * value_rows
    upstream = cotangent * queries
    stacked = jnp.stack([filters, inner, upstream], axis=1)
    whole_length = lax.all_to_all(stacked, "seq", split_axis=2, concat_axis=0, tiled=True)
    results = local_convolve(whole_length)
    returned = lax.all_to_all(results, "seq", split_axis=0, concat_axis=2, tiled=True)
    conv = returned[:, 0]
    grad_inner = returned[:, 1]
    filter_raw = returned[:, 2]
    output = queries * conv
    filter_grad = filter_raw * scale_factor
    branch_grads = jnp.stack(
        [cotangent * conv, grad_inner * value_rows, grad_inner * key_rows], axis=1
    ).astype(jnp.bfloat16)
    one_hot = (token_ids[:, None] == lax.iota(jnp.int32, vocabulary)[None, :]).astype(jnp.bfloat16)
    token_sums = lax.dot_general(
        one_hot,
        branch_grads.reshape(tok_count, branches * width),
        (((0,), (0,)), ((), ())),
        preferred_element_type=jnp.float32,
    )
    summed = summed_on_arrival(token_sums.reshape(vocabulary, branches, width), "seq", 2)
    gathered = gather_directly(summed[:, :, None, :], "red", 2)
    weight_grad = (
        lax.dot_general(
            embedding.astype(jnp.float32),
            gathered.reshape(vocabulary, branches * red_count * piece),
            (((0,), (0,)), ((), ())),
            precision=precise_mode,
        )
        * scale_factor
    )
    return (
        output,
        filter_grad,
        branch_grads,
        weight_grad.reshape(width_rows, branches, red_count, piece),
    )


def solution(mesh):
    in_specs = (
        P("seq"),
        P(None, "red"),
        P("red", None, None, "seq"),
        P("seq", "red"),
        P("seq", "red"),
    )
    out_specs = (
        P("seq", "red"),
        P("seq", "red"),
        P("seq", None, "red"),
        P("red", None, None, "seq"),
    )
    return jax.shard_map(shards, mesh=mesh, in_specs=in_specs, out_specs=out_specs, check_vma=False)
```

profile of v0, /device:TPU:1, one launch (start us, length us, event | category | flops | bytes accessed | tf_op | source)
XLA Modules:
  0.0 240.9 jit_solution(10747169346815855003)
XLA Ops:
  2.4 9.0 %all_to_all.53 = f32[4,512,3,1,4]{1,4,2,3,0:T(4,128)S(1)} all-to-all(f32[4,512,3,1,4]{1,4,2,3,0:T(4,128)S(1)} %copy.50), channel_id=1, replica_groups=mesh['seq'=64,'red'=4] {'red'}, dimensions={0} | all-to-all | bytes 196608 | tf_op jit(solution)/shard_map/all_to_all | solution.py:17
  11.4 1.4 broadcast_in_dim.17
  12.7 12.7 %all-to-all-start.1 = ((f32[64,512,3,1,4]{1,4,2,3,0:T(4,128)}), f32[64,512,3,1,4]{1,4,2,3,0:T(4,128)S(1)}, u32[]{:S(2)}, u32[]{:S(2)}) async-start(f32[64,512,3,1,4]{1,4,2,3,0:T(4,128)} %broadcast_in_dim.17), calls=%async_computation.1 | async-start | bytes 3145728 | tf_op jit(solution)/shard_map/all_to_all | solution.py:23
  25.6 39.4 %all-to-all-done.1 = f32[64,512,3,1,4]{1,4,2,3,0:T(4,128)S(1)} async-done(((f32[64,512,3,1,4]{1,4,2,3,0:T(4,128)}), f32[64,512,3,1,4]{1,4,2,3,0:T(4,128)S(1)}, u32[]{:S(2)}, u32[]{:S(2)}) %all-to-all-start.1) | async-done | bytes 1572896 | tf_op jit(solution)/shard_map/all_to_all | solution.py:23
  65.0 1.5 copy.51
  66.5 1.8 reshape.123
  68.3 1.8 copy.52
  70.1 2.5 %gather_fusion = f32[128,3,256]{2,1,0:T(4,128)S(1)} fusion(f32[512,3,256]{2,1,0:T(4,128)} %copy.52, s32[1024]{0:T(1024)S(1)} %pad_clamp_fusion), kind=kCustom, calls=%fused_computation | custom fusion | bytes 786944 | tf_op jit(solution)/shard_map/jit(_take)/gather | solution.py:145
  74.6 8.6 %all-to-all-start.2 = ((f32[128,3,256]{0,1,2:T(4,128)}), f32[128,3,256]{0,1,2:T(4,128)S(1)}, u32[]{:S(2)}, u32[]{:S(2)}) async-start(f32[128,3,256]{0,1,2:T(4,128)} %copy.54), calls=%async_computation.2 | async-start | bytes 1048576 | tf_op jit(solution)/shard_map/all_to_all | solution.py:153
  83.8 14.8 %all-to-all-done.2 = f32[128,3,256]{0,1,2:T(4,128)S(1)} async-done(((f32[128,3,256]{0,1,2:T(4,128)}), f32[128,3,256]{0,1,2:T(4,128)S(1)}, u32[]{:S(2)}, u32[]{:S(2)}) %all-to-all-start.2) | async-done | bytes 393248 | tf_op jit(solution)/shard_map/all_to_all | solution.py:153
  99.4 1.1 fusion.4
  110.0 1.3 fusion.10
  111.4 1.1 fusion.8
  112.7 10.7 %copy.57 = f32[8192,3,4]{2,1,0:T(4,128)} copy(f32[8192,3,4]{0,2,1:T(4,128)S(1)} %div.10) | data formatting | bytes 786432 | tf_op jit(solution)/shard_map/div | solution.py:126
  123.3 16.0 %reshape.142 = f32[64,1,1536]{2,1,0:T(1,128)S(1)} reshape(f32[8192,3,4]{2,1,0:T(4,128)} %copy.57) | data formatting | bytes 786432
  139.4 19.7 %all_to_all.54 = f32[64,1,1536]{2,1,0:T(1,128)S(1)} all-to-all(f32[64,1,1536]{2,1,0:T(1,128)S(1)} %reshape.142), channel_id=1, replica_groups=mesh['seq'=64,'red'=4] {'seq'}, dimensions={0} | all-to-all | bytes 786432 | tf_op jit(solution)/shard_map/all_to_all | solution.py:155
  159.6 1.6 reduce.1
  161.1 11.5 %reshape.143 = f32[8192,3,4]{2,1,0:T(4,128)} reshape(f32[64,1536]{1,0:T(8,128)S(1)} %reduce.1) | data formatting | bytes 786432
  172.6 11.7 %copy.58 = f32[64,128,3,4]{1,3,0,2:T(4,128)S(1)} copy(f32[64,128,3,4]{3,2,1,0:T(4,128)} %bitcast.114) | data formatting | bytes 786432 | tf_op jit(solution)/shard_map/all_to_all | solution.py:155
  186.2 2.2 copy.64
  188.4 5.3 %all-to-all-start.4 = ((f32[64,512,3,4]{1,3,2,0:T(4,128)}), f32[64,512,3,4]{1,3,2,0:T(4,128)S(1)}, u32[]{:S(2)}, u32[]{:S(2)}) async-start(f32[64,512,3,4]{1,3,2,0:T(4,128)} %copy.64), calls=%async_computation.4 | async-start | bytes 3145728 | tf_op jit(solution)/shard_map/all_to_all | solution.py:17
  195.2 27.0 %all-to-all-done.4 = f32[64,512,3,4]{1,3,2,0:T(4,128)S(1)} async-done(((f32[64,512,3,4]{1,3,2,0:T(4,128)}), f32[64,512,3,4]{1,3,2,0:T(4,128)S(1)}, u32[]{:S(2)}, u32[]{:S(2)}) %all-to-all-start.4) | async-done | bytes 1572896 | tf_op jit(solution)/shard_map/all_to_all | solution.py:17
  223.0 13.1 %all-to-all-start.5 = ((f32[4,512,3,1,4]{1,4,2,3,0:T(4,128)}), f32[4,512,3,1,4]{1,4,2,3,0:T(4,128)S(1)}, u32[]{:S(2)}, u32[]{:S(2)}) async-start(f32[4,512,3,1,4]{1,4,2,3,0:T(4,128)} %broadcast_in_dim.20), calls=%async_computation.5 | async-start | bytes 196608 | tf_op jit(solution)/shard_map/all_to_all | solution.py:23
  236.8 2.7 %all-to-all-done.5 = f32[4,512,3,1,4]{1,4,2,3,0:T(4,128)S(1)} async-done(((f32[4,512,3,1,4]{1,4,2,3,0:T(4,128)}), f32[4,512,3,1,4]{1,4,2,3,0:T(4,128)S(1)}, u32[]{:S(2)}, u32[]{:S(2)}) %all-to-all-start.5) | async-done | bytes 98336 | tf_op jit(solution)/shard_map/all_to_all | solution.py:23
  (63 shorter events, 21.5 us)
Async XLA Ops:
  0.6 1.3 copy-start
  12.7 12.7 %copy-start.2 = (f32[128,256]{1,0:T(8,128)S(1)}, f32[128,256]{1,0:T(8,128)}, u32[]{:S(2)}) copy-start(f32[128,256]{1,0:T(8,128)} %param.8) | copy-start | bytes 393220
  12.7 12.8 %copy-start.3 = (s32[128]{0:T(128)S(1)}, s32[128]{0:T(128)}, u32[]{:S(2)}) copy-start(s32[128]{0:T(128)} %param.5) | copy-start | bytes 1540
  12.7 52.2 %all-to-all-start.1 = ((f32[64,512,3,1,4]{1,4,2,3,0:T(4,128)}), f32[64,512,3,1,4]{1,4,2,3,0:T(4,128)S(1)}, u32[]{:S(2)}, u32[]{:S(2)}) async-start(f32[64,512,3,1,4]{1,4,2,3,0:T(4,128)} %broadcast_in_dim.17), calls=%async_computation.1 | async-start | bytes 3145728 | tf_op jit(solution)/shard_map/all_to_all | solution.py:23
  70.1 3.0 %copy-start.1 = (f32[128,256]{1,0:T(8,128)S(1)}, f32[128,256]{1,0:T(8,128)}, u32[]{:S(2)}) copy-start(f32[128,256]{1,0:T(8,128)} %param.9) | copy-start | bytes 393220
  74.6 24.1 %all-to-all-start.2 = ((f32[128,3,256]{0,1,2:T(4,128)}), f32[128,3,256]{0,1,2:T(4,128)S(1)}, u32[]{:S(2)}, u32[]{:S(2)}) async-start(f32[128,3,256]{0,1,2:T(4,128)} %copy.54), calls=%async_computation.2 | async-start | bytes 1048576 | tf_op jit(solution)/shard_map/all_to_all | solution.py:153
  188.4 33.7 %all-to-all-start.4 = ((f32[64,512,3,4]{1,3,2,0:T(4,128)}), f32[64,512,3,4]{1,3,2,0:T(4,128)S(1)}, u32[]{:S(2)}, u32[]{:S(2)}) async-start(f32[64,512,3,4]{1,3,2,0:T(4,128)} %copy.64), calls=%async_computation.4 | async-start | bytes 3145728 | tf_op jit(solution)/shard_map/all_to_all | solution.py:17
  223.0 16.4 %all-to-all-start.5 = ((f32[4,512,3,1,4]{1,4,2,3,0:T(4,128)}), f32[4,512,3,1,4]{1,4,2,3,0:T(4,128)S(1)}, u32[]{:S(2)}, u32[]{:S(2)}) async-start(f32[4,512,3,1,4]{1,4,2,3,0:T(4,128)} %broadcast_in_dim.20), calls=%async_computation.5 | async-start | bytes 196608 | tf_op jit(solution)/shard_map/all_to_all | solution.py:23
where the time goes:
time: 242 us; the launch traced here: 241 us
  waiting for transfers between devices  83.9 us (35%)
  local copies, waits for them, and re-layouts  68.4 us (28%)
  starting transfers between devices  39.7 us (16%)
  blocking collectives  28.6 us (12%)
  matrix products  14.3 us (6%)
  other arithmetic  4.98 us (2%)
    all_to_all x2, waiting for transfers between devices, copy_for_each(): lax.all_to_all(jnp.broadcast_to(value[None], (length, *value.shape)), axi...  42.1 us
    unnamed x17, local copies, waits for them, and re-layouts  30 us
    all_to_all x1, waiting for transfers between devices, summed_on_arrival(): lax.all_to_all(tiles, axis, split_axis=0, concat_axis=0, tiled=True)  27 us
    all_to_all x2, starting transfers between devices, copy_for_each(): lax.all_to_all(jnp.broadcast_to(value[None], (length, *value.shape)), axi...  25.7 us
    all_to_all x1, blocking collectives, shards(): lax.all_to_all(results, 'seq', split_axis=0, concat_axis=2, tiled=True)  19.7 us
    all_to_all x1, waiting for transfers between devices, shards(): lax.all_to_all(stacked, 'seq', split_axis=2, concat_axis=0, tiled=True)  14.8 us
    all_to_all x2, local copies, waits for them, and re-layouts, shards(): lax.all_to_all(results, 'seq', split_axis=0, concat_axis=2, tiled=True)  12.2 us
    div x2, local copies, waits for them, and re-layouts, local_convolve(): result = result.reshape(total, branch_count * narrow)[:length] / total  10.8 us
  transfers between devices with their start and end apart: 4, of which 4 were waited for; matrix products, arithmetic and copies ran while one was open for 1% of the time, Pallas kernels for 0%

commit v1 on v0

--- a/solution.py
+++ b/solution.py
@@ -152,7 +152,10 @@
     stacked = jnp.stack([filters, inner, upstream], axis=1)
     whole_length = lax.all_to_all(stacked, "seq", split_axis=2, concat_axis=0, tiled=True)
     results = local_convolve(whole_length)
-    returned = lax.all_to_all(results, "seq", split_axis=0, concat_axis=2, tiled=True)
+    returned = jnp.concatenate(
+        lax.all_to_all(jnp.stack(jnp.split(results, lax.axis_size("seq"), axis=0)), "seq", 0, 0),
+        axis=2,
+    )
     conv = returned[:, 0]
     grad_inner = returned[:, 1]
     filter_raw = returned[:, 2]

time: 242 us -> 190 us (0.79)
  local copies, waits for them, and re-layouts: 68.4 us -> 18.7 us
    unnamed x17 -> x78, local copies, waits for them, and re-layouts: 30 us -> 2.99 us
    all_to_all x2 -> x0, local copies, waits for them, and re-layouts: 12.2 us -> none  [shards(): lax.all_to_all(results, 'seq', split_axis=0, concat_axis=2, tiled=True)]
    div x2 -> x0, local copies, waits for them, and re-layouts: 10.8 us -> none  [local_convolve(): result = result.reshape(total, branch_count * narrow)[:length] / total]
where the time goes in v1:
time: 190 us
  waiting for transfers between devices  83.9 us (44%)
  starting transfers between devices  39.7 us (21%)
  blocking collectives  28.6 us (15%)
  local copies, waits for them, and re-layouts  18.7 us (10%)
  matrix products  14.3 us (8%)
  other arithmetic  3.41 us (2%)
    all_to_all x2, waiting for transfers between devices, copy_for_each(): lax.all_to_all(jnp.broadcast_to(value[None], (length, *value.shape)), axi...  42.1 us
    all_to_all x1, waiting for transfers between devices, summed_on_arrival(): lax.all_to_all(tiles, axis, split_axis=0, concat_axis=0, tiled=True)  27 us
    all_to_all x2, starting transfers between devices, copy_for_each(): lax.all_to_all(jnp.broadcast_to(value[None], (length, *value.shape)), axi...  25.7 us
    all_to_all x1, blocking collectives, shards(): lax.all_to_all(jnp.stack(jnp.split(results, lax.axis_size('seq'), axis=0)...  19.7 us
    all_to_all x1, waiting for transfers between devices, shards(): lax.all_to_all(stacked, 'seq', split_axis=2, concat_axis=0, tiled=True)  14.8 us
    all_to_all x1, blocking collectives, summed_on_arrival(): lax.all_to_all(tiles, axis, split_axis=0, concat_axis=0, tiled=True)  8.96 us
    all_to_all x1, starting transfers between devices, shards(): lax.all_to_all(stacked, 'seq', split_axis=2, concat_axis=0, tiled=True)  8.64 us
    all_to_all x1, starting transfers between devices, summed_on_arrival(): lax.all_to_all(tiles, axis, split_axis=0, concat_axis=0, tiled=True)  5.29 us
  transfers between devices with their start and end apart: 4, of which 4 were waited for; matrix products, arithmetic and copies ran while one was open for 1% of the time, Pallas kernels for 0%

profile of v1, /device:TPU:1, one launch (start us, length us, event | category | flops | bytes accessed | tf_op | source)
XLA Modules:
  0.0 189.9 jit_solution(4155411068539028775)
XLA Ops:
  2.4 9.0 %all_to_all.40 = f32[4,512,3,1,4]{1,4,2,3,0:T(4,128)S(1)} all-to-all(f32[4,512,3,1,4]{1,4,2,3,0:T(4,128)S(1)} %copy.177), channel_id=1, replica_groups=mesh['seq'=64,'red'=4] {'red'}, dimensions={0} | all-to-all | bytes 196608 | tf_op jit(solution)/shard_map/all_to_all | solution.py:17
  11.4 1.4 broadcast_in_dim.17
  12.8 12.7 %all-to-all-start.1 = ((f32[64,512,3,1,4]{1,4,2,3,0:T(4,128)}), f32[64,512,3,1,4]{1,4,2,3,0:T(4,128)S(1)}, u32[]{:S(2)}, u32[]{:S(2)}) async-start(f32[64,512,3,1,4]{1,4,2,3,0:T(4,128)} %broadcast_in_dim.17), calls=%async_computation.1 | async-start | bytes 3145728 | tf_op jit(solution)/shard_map/all_to_all | solution.py:23
  25.6 39.4 %all-to-all-done.1 = f32[64,512,3,1,4]{1,4,2,3,0:T(4,128)S(1)} async-done(((f32[64,512,3,1,4]{1,4,2,3,0:T(4,128)}), f32[64,512,3,1,4]{1,4,2,3,0:T(4,128)S(1)}, u32[]{:S(2)}, u32[]{:S(2)}) %all-to-all-start.1) | async-done | bytes 1572896 | tf_op jit(solution)/shard_map/all_to_all | solution.py:23
  65.0 1.5 copy.178
  66.5 1.8 reshape.386
  68.3 1.8 copy.179
  70.1 2.5 %gather_fusion = f32[128,3,256]{2,1,0:T(4,128)S(1)} fusion(f32[512,3,256]{2,1,0:T(4,128)} %copy.179, s32[1024]{0:T(1024)S(1)} %pad_clamp_fusion), kind=kCustom, calls=%fused_computation | custom fusion | bytes 786944 | tf_op jit(solution)/shard_map/jit(_take)/gather | solution.py:145
  73.6 1.0 copy.181
  74.6 8.6 %all-to-all-start.2 = ((f32[128,3,256]{0,1,2:T(4,128)}), f32[128,3,256]{0,1,2:T(4,128)S(1)}, u32[]{:S(2)}, u32[]{:S(2)}) async-start(f32[128,3,256]{0,1,2:T(4,128)} %copy.181), calls=%async_computation.2 | async-start | bytes 1048576 | tf_op jit(solution)/shard_map/all_to_all | solution.py:153
  83.9 14.8 %all-to-all-done.2 = f32[128,3,256]{0,1,2:T(4,128)S(1)} async-done(((f32[128,3,256]{0,1,2:T(4,128)}), f32[128,3,256]{0,1,2:T(4,128)S(1)}, u32[]{:S(2)}, u32[]{:S(2)}) %all-to-all-start.2) | async-done | bytes 393248 | tf_op jit(solution)/shard_map/all_to_all | solution.py:153
  99.4 1.1 fusion.4
  100.5 1.1 fusion.6
  102.6 1.0 fusion.31
  103.6 1.0 fusion.1
  104.7 1.0 fusion
  110.1 1.3 fusion.10
  111.4 1.1 fusion.8
  113.6 19.7 %all_to_all.41 = f32[64,128,3,4]{1,3,2,0:T(4,128)S(1)} all-to-all(f32[64,128,3,4]{1,3,2,0:T(4,128)S(1)} %constant_dynamic-update-slice_fusion), channel_id=1, replica_groups=mesh['seq'=64,'red'=4] {'seq'}, dimensions={0} | all-to-all | bytes 786432 | tf_op jit(solution)/shard_map/all_to_all | solution.py:156
  135.2 2.2 %copy.190 = f32[64,512,3,4]{1,3,2,0:T(4,128)} copy(f32[64,512,3,4]{1,0,3,2:T(8,128)S(1)} %convolution_bitcast_fusion) | data formatting | bytes 3145728 | tf_op jit(solution)/shard_map/transpose | solution.py:12
  137.4 5.3 %all-to-all-start.4 = ((f32[64,512,3,4]{1,3,2,0:T(4,128)}), f32[64,512,3,4]{1,3,2,0:T(4,128)S(1)}, u32[]{:S(2)}, u32[]{:S(2)}) async-start(f32[64,512,3,4]{1,3,2,0:T(4,128)} %copy.190), calls=%async_computation.4 | async-start | bytes 3145728 | tf_op jit(solution)/shard_map/all_to_all | solution.py:17
  144.2 27.0 %all-to-all-done.4 = f32[64,512,3,4]{1,3,2,0:T(4,128)S(1)} async-done(((f32[64,512,3,4]{1,3,2,0:T(4,128)}), f32[64,512,3,4]{1,3,2,0:T(4,128)S(1)}, u32[]{:S(2)}, u32[]{:S(2)}) %all-to-all-start.4) | async-done | bytes 1572896 | tf_op jit(solution)/shard_map/all_to_all | solution.py:17
  172.0 13.0 %all-to-all-start.5 = ((f32[4,512,3,1,4]{1,4,2,3,0:T(4,128)}), f32[4,512,3,1,4]{1,4,2,3,0:T(4,128)S(1)}, u32[]{:S(2)}, u32[]{:S(2)}) async-start(f32[4,512,3,1,4]{1,4,2,3,0:T(4,128)} %broadcast_in_dim.20), calls=%async_computation.5 | async-start | bytes 196608 | tf_op jit(solution)/shard_map/all_to_all | solution.py:23
  185.8 2.7 %all-to-all-done.5 = f32[4,512,3,1,4]{1,4,2,3,0:T(4,128)S(1)} async-done(((f32[4,512,3,1,4]{1,4,2,3,0:T(4,128)}), f32[4,512,3,1,4]{1,4,2,3,0:T(4,128)S(1)}, u32[]{:S(2)}, u32[]{:S(2)}) %all-to-all-start.5) | async-done | bytes 98336 | tf_op jit(solution)/shard_map/all_to_all | solution.py:23
  (125 shorter events, 16.5 us)
Async XLA Ops:
  0.6 1.3 copy-start
  12.7 12.7 %copy-start.2 = (f32[128,256]{1,0:T(8,128)S(1)}, f32[128,256]{1,0:T(8,128)}, u32[]{:S(2)}) copy-start(f32[128,256]{1,0:T(8,128)} %param.8) | copy-start | bytes 393220
  12.8 12.8 %copy-start.3 = (s32[128]{0:T(128)S(1)}, s32[128]{0:T(128)}, u32[]{:S(2)}) copy-start(s32[128]{0:T(128)} %param.5) | copy-start | bytes 1540
  12.8 52.2 %all-to-all-start.1 = ((f32[64,512,3,1,4]{1,4,2,3,0:T(4,128)}), f32[64,512,3,1,4]{1,4,2,3,0:T(4,128)S(1)}, u32[]{:S(2)}, u32[]{:S(2)}) async-start(f32[64,512,3,1,4]{1,4,2,3,0:T(4,128)} %broadcast_in_dim.17), calls=%async_computation.1 | async-start | bytes 3145728 | tf_op jit(solution)/shard_map/all_to_all | solution.py:23
  70.1 3.0 %copy-start.1 = (f32[128,256]{1,0:T(8,128)S(1)}, f32[128,256]{1,0:T(8,128)}, u32[]{:S(2)}) copy-start(f32[128,256]{1,0:T(8,128)} %param.9) | copy-start | bytes 393220
  74.6 24.1 %all-to-all-start.2 = ((f32[128,3,256]{0,1,2:T(4,128)}), f32[128,3,256]{0,1,2:T(4,128)S(1)}, u32[]{:S(2)}, u32[]{:S(2)}) async-start(f32[128,3,256]{0,1,2:T(4,128)} %copy.181), calls=%async_computation.2 | async-start | bytes 1048576 | tf_op jit(solution)/shard_map/all_to_all | solution.py:153
  137.4 33.7 %all-to-all-start.4 = ((f32[64,512,3,4]{1,3,2,0:T(4,128)}), f32[64,512,3,4]{1,3,2,0:T(4,128)S(1)}, u32[]{:S(2)}, u32[]{:S(2)}) async-start(f32[64,512,3,4]{1,3,2,0:T(4,128)} %copy.190), calls=%async_computation.4 | async-start | bytes 3145728 | tf_op jit(solution)/shard_map/all_to_all | solution.py:17
  172.0 16.4 %all-to-all-start.5 = ((f32[4,512,3,1,4]{1,4,2,3,0:T(4,128)}), f32[4,512,3,1,4]{1,4,2,3,0:T(4,128)S(1)}, u32[]{:S(2)}, u32[]{:S(2)}) async-start(f32[4,512,3,1,4]{1,4,2,3,0:T(4,128)} %broadcast_in_dim.20), calls=%async_computation.5 | async-start | bytes 196608 | tf_op jit(solution)/shard_map/all_to_all | solution.py:23
